TPU v7x, 32 devices: a whole 2x2x4 slice. The times are simulated.
32 devices in a mesh: shot: 2 (over y), space: 16 (over z, x, core).
Axes of the slice: x: 2, y: 2, z: 4, core: 2. Of those that a mesh axis runs over, the one named last changes fastest.
Arguments:
- wave_prev: float32 [2, 256, 128, 128], P('shot', 'space'), may hold values from -6 to 6
- wave_now: float32 [2, 256, 128, 128], P('shot', 'space'), may hold values from -6 to 6
- velocity: float32 [256, 128, 128], P('space'), may hold values from 0.05 to 0.2
- probe_panel: float32 [4, 256, 128, 128], P(None, 'space', 'shot'), may hold values from -6 to 6
- source_depth: int32 [2], P('shot'), may hold values from 0 to 255
- source_column: int32 [2], P('shot'), may hold values from 0 to 16383
- source_strength: float32 [2], P('shot'), may hold values from 2 to 6
- receiver_wells: int32 [2, 512], P('shot'), may hold values from 0 to 16383
Outputs:
- hessian_action: float32 [4, 256, 128, 128], P(None, 'space', 'shot')
All inputs are finite; a program needn't handle non-finite values.
Results may differ from a plain program's by a relative error of at most 0.0003.
Values sent between devices are 32-bit elements; how exact they have to be, the bound alone decides.
A program may use at most 128 MiB of HBM per device.

v0:
```python
import jax
import jax.numpy as jnp
from jax import lax
from jax.sharding import PartitionSpec as P

CENTER = -205.0 / 72.0
WEIGHTS = (8.0 / 5.0, -1.0 / 5.0, 8.0 / 315.0, -1.0 / 560.0)


def extended(block, sides, width):
    for axis, dim in sides:
        count = lax.axis_size(axis)
        forward = [(i, i + 1) for i in range(count - 1)]
        backward = [(target, source) for source, target in forward]
        low = lax.ppermute(
            lax.slice_in_dim(block, block.shape[dim] - width, None, axis=dim), axis, forward
        )
        high = lax.ppermute(lax.slice_in_dim(block, 0, width, axis=dim), axis, backward)
        block = jnp.concatenate([low, block, high], axis=dim)
    return block


def laplace(padded):
    count_rows = padded.shape[-3] - 8
    middle = padded[..., 4 : 4 + count_rows, :, :]
    count_x = middle.shape[-2]
    count_y = middle.shape[-1]
    lead_pads = [(0, 0)] * (middle.ndim - 2)
    wide_x = jnp.pad(middle, lead_pads + [(4, 4), (0, 0)])
    wide_y = jnp.pad(middle, lead_pads + [(0, 0), (4, 4)])
    stencil = 3.0 * CENTER * middle
    for offset in range(1, 5):
        weight = WEIGHTS[offset - 1]
        stencil = stencil + weight * (
            padded[..., 4 + offset : 4 + offset + count_rows, :, :]
            + padded[..., 4 - offset : 4 - offset + count_rows, :, :]
        )
        stencil = stencil + weight * (
            wide_x[..., 4 + offset : 4 + offset + count_x, :]
            + wide_x[..., 4 - offset : 4 - offset + count_x, :]
        )
        stencil = stencil + weight * (
            wide_y[..., 4 + offset : 4 + offset + count_y]
            + wide_y[..., 4 - offset : 4 - offset + count_y]
        )
    return stencil


def tally(wells, columns):
    return jnp.zeros((columns,), jnp.float32).at[wells].add(1.0)


def per_device(
    wave_prev,
    wave_now,
    velocity,
    probe_panel,
    source_depth,
    source_column,
    source_strength,
    receiver_wells,
):
    shot_count = wave_now.shape[0]
    count_z = wave_now.shape[1]
    width_x = wave_now.shape[2]
    width_y = wave_now.shape[3]
    probe_count = probe_panel.shape[0]
    columns = width_x * width_y
    probes = lax.all_gather(probe_panel, "shot", axis=2, tiled=True)
    first_row = lax.axis_index("space") * count_z
    column_ids = jnp.arange(columns, dtype=jnp.int32).reshape(width_x, width_y)
    now_wide = extended(wave_now, (("space", 1),), 4)
    born_zero = velocity * laplace(now_wide)
    depth_rows = first_row + jnp.arange(count_z, dtype=jnp.int32)
    hit_depth = depth_rows[None, :] == source_depth[:, None]
    hit_column = column_ids[None, :, :] == source_column[:, None, None]
    marks = (hit_depth[:, :, None, None] & hit_column[:, None, :, :]).astype(jnp.float32)
    upcoming = 2.0 * wave_now - wave_prev + born_zero + marks * source_strength[:, None, None, None]
    next_wide = extended(upcoming, (("space", 1),), 4)
    born_one = velocity * laplace(next_wide)
    first_field = probes[:, None] * born_zero[None]
    flat_first = first_field.reshape(probe_count * shot_count, count_z, width_x, width_y)
    first_wide = extended(flat_first, (("space", 1),), 4)
    first_wide = first_wide.reshape(probe_count, shot_count, count_z + 8, width_x, width_y)
    second_field = (
        2.0 * first_field + velocity * laplace(first_wide) + probes[:, None] * born_one[None]
    )
    counts = jax.vmap(lambda wells: tally(wells, columns))(receiver_wells)
    counts = counts.reshape(shot_count, width_x, width_y)[None, :, None]
    late_field = counts * second_field
    weighted = velocity * late_field
    flat_weighted = weighted.reshape(probe_count * shot_count, count_z, width_x, width_y)
    weighted_wide = extended(flat_weighted, (("space", 1),), 4)
    weighted_wide = weighted_wide.reshape(probe_count, shot_count, count_z + 8, width_x, width_y)
    early_field = counts * first_field + 2.0 * late_field + laplace(weighted_wide)
    local_sum = jnp.sum(born_zero[None] * early_field + born_one[None] * late_field, axis=1)
    summed = lax.psum_scatter(local_sum, "shot", scatter_dimension=2, tiled=True)
    return summed / (shot_count * lax.axis_size("shot"))


def solution(mesh):
    return jax.shard_map(
        per_device,
        mesh=mesh,
        in_specs=(
            P("shot", "space", None, None),
            P("shot", "space", None, None),
            P("space", None, None),
            P(None, "space", "shot", None),
            P("shot"),
            P("shot"),
            P("shot"),
            P("shot", None),
        ),
        out_specs=P(None, "space", "shot", None),
        check_vma=False,
    )
```

profile of v0, /device:TPU:9, one launch (start us, length us, event | category | flops | bytes accessed | tf_op | source)
XLA Modules:
  0.0 315.2 jit_solution(11887566937880154067)
XLA Ops:
  6.5 0.0 all-gather.2.cloned.1.call-start
  6.5 0.7 all-gather.2.cloned.1.call-update
  7.3 0.0 reduce-scatter.2.cloned.1.call-start
  7.3 1.1 fusion.131
  8.4 2.6 collective-permute-start
  11.0 3.0 collective-permute-start.1
  15.3 0.0 copy-start.7
  16.1 0.7 fusion.125
  16.8 2.3 collective-permute-done.1
  19.1 0.0 copy-done.5
  19.1 0.2 constant_dynamic-update-slice_fusion.1
  19.3 0.0 collective-permute-done
  19.4 0.0 copy-done.4
  19.4 3.7 %select_add_fusion = (f32[1,16,128,128]{3,2,1,0:T(8,128)}, f32[1,16,128,128]{3,2,1,0:T(8,128)S(1)}) fusion(f32[1,16,128,128]{3,2,1,0:T(8,128)S(1)} %copy-done.7, f32[1,16,128,128]{3,2,1,0:T(8,128)S(1)} %copy-done.5, f32[]{:T(128)} %bitcast.42, pred[128,128]{1,0:T(8,128)(4,1)S(1)} %add_compare_fusion, pred[16]{0:T(512)(128)(4,1)S(1)} %add_compare_fusion.1, ...), kind=kLoop, calls=%fused_computation.196 | loop fusion | flops 11534336 | bytes 13647892 | tf_op jit(solution)/shard_map/add | solution.py:78
  23.1 43.8 %all-gather.2.cloned.1.call-done = f32[4,16,128,128]{3,2,1,0:T(8,128)} async-done(((f32[4,16,64,128]{3,2,1,0:T(8,128)}), f32[4,16,128,128]{3,2,1,0:T(8,128)}) %all-gather.2.cloned.1.call-update) | async-done | bytes 4194320 | tf_op jit(solution)/shard_map/all_gather | solution.py:69
  66.9 2.6 broadcast_multiply_fusion
  69.5 0.0 copy-start.3
  69.5 1.9 copy-done.3
  71.4 1.5 fusion.129
  72.9 3.6 %collective-permute-start.2 = (f32[4,4,128,128]{3,2,1,0:T(8,128)}, f32[4,4,128,128]{3,2,1,0:T(8,128)}, u32[]{:S(2)}, u32[]{:S(2)}) collective-permute-start(f32[4,4,128,128]{3,2,1,0:T(8,128)} %get-tuple-element.11), channel_id=1, source_target_pairs={{0,1},{1,2},{2,3},{3,4},{4,5},{5,6},{6,7},{7,8},{8,9},{9,10},{10,1... | collective-permute-start | bytes 3145736 | tf_op jit(solution)/shard_map/ppermute | solution.py:15
  76.6 1.9 collective-permute-start.3
  78.5 0.0 copy-done.6
  78.5 0.9 fusion.130
  79.4 3.5 %collective-permute-start.4 = (f32[1,4,128,128]{3,2,1,0:T(8,128)}, f32[1,4,128,128]{3,2,1,0:T(8,128)S(1)}, u32[]{:S(2)}, u32[]{:S(2)}) collective-permute-start(f32[1,4,128,128]{3,2,1,0:T(8,128)} %get-tuple-element.13), channel_id=1, source_target_pairs={{1,0},{2,1},{3,2},{4,3},{5,4},{6,5},{7,6},{8,7},{9,8},{10,9},{11,1... | collective-permute-start | bytes 786440 | tf_op jit(solution)/shard_map/ppermute | solution.py:18
  82.8 2.1 collective-permute-start.5
  85.0 3.3 %scatter_custom_fusion = f32[16384]{0:T(1024)S(1)} fusion(s32[512]{0:T(512)S(1)} %bitcast.48, f32[512]{0:T(512)S(1)} %broadcast.143, f32[]{:T(128)} %constant.16.clone.1), kind=kCustom, calls=%fused_computation.199 | custom fusion | flops 512 | bytes 65540 | tf_op jit(solution)/shard_map/vmap()/scatter-add | solution.py:50
  88.3 18.7 %collective-permute-done.4 = f32[1,4,128,128]{3,2,1,0:T(8,128)S(1)} collective-permute-done((f32[1,4,128,128]{3,2,1,0:T(8,128)}, f32[1,4,128,128]{3,2,1,0:T(8,128)S(1)}, u32[]{:S(2)}, u32[]{:S(2)}) %collective-permute-start.4) | collective-permute-done | bytes 262176 | tf_op jit(solution)/shard_map/ppermute | solution.py:18
  107.0 0.0 collective-permute-done.5
  107.0 15.7 %fusion.66 = f32[16,128,128]{2,1,0:T(8,128)S(1)} fusion(f32[1,16,128,128]{3,2,1,0:T(8,128)} %get-tuple-element.7, f32[1,4,128,128]{3,2,1,0:T(8,128)} %collective-permute-done.5, f32[1,4,128,128]{3,2,1,0:T(8,128)S(1)} %collective-permute-done.4, f32[16,128,128]{2,1,0:T(8,128)S(1)} %copy-done.4), kind=kLoop, calls=%fused_computation.126 | loop fusion | flops 12058624 | bytes 3670016 | tf_op jit(solution)/shard_map/mul | solution.py:86
  122.7 0.0 collective-permute-done.2
  122.7 0.0 collective-permute-done.3
  122.7 3.2 %maximum_bitcast_fusion = f32[4,1,24,128,128]{4,3,2,0,1:T(8,128)S(1)} fusion(f32[4,4,128,128]{3,2,1,0:T(8,128)} %collective-permute-done.3, f32[4,16,128,128]{3,2,1,0:T(8,128)} %copy-done.3, f32[4,4,128,128]{3,2,1,0:T(8,128)} %collective-permute-done.2), kind=kLoop, calls=%fused_computation.17 | loop fusion | flops 3145728 | bytes 12582912 | tf_op jit(solution)/shard_map/reshape | solution.py:84
  126.0 2.4 slice.454
  128.4 1.5 copy-done.1
  129.8 42.2 %multiply_bitcast_fusion = (f32[4,16,128,128]{3,2,1,0:T(8,128)}, f32[4,1,16,128,128]{4,3,2,0,1:T(8,128)}) fusion(f32[16,128,128]{2,1,0:T(8,128)S(1)} %copy-done.4, f32[4,16,128,128]{3,2,1,0:T(8,128)} %all-gather.2.cloned.1.call-done, f32[16,128,128]{2,1,0:T(8,128)S(1)} %fusion.66, f32[4,1,24,128,128]{4,3,2,0,1:T(8,128)} %copy-done.1, ...), kind=kLoop, calls=%fused_computation.99 | loop fusion | flops 47185920 | bytes 53542912 | tf_op jit(solution)/shard_map/reshape | solution.py:92
  172.1 1.8 fusion.128
  173.9 3.0 collective-permute-start.6
  177.0 2.1 collective-permute-start.7
  179.1 20.8 %collective-permute-done.6 = f32[4,4,128,128]{3,2,1,0:T(8,128)S(1)} collective-permute-done((f32[4,4,128,128]{3,2,1,0:T(8,128)S(1)}, f32[4,4,128,128]{3,2,1,0:T(8,128)S(1)}, u32[]{:S(2)}, u32[]{:S(2)}) %collective-permute-start.6) | collective-permute-done | bytes 1048608 | tf_op jit(solution)/shard_map/ppermute | solution.py:15
  199.9 0.0 collective-permute-done.7
  199.9 0.8 maximum_bitcast_fusion.1
  200.7 0.0 copy-start
  200.7 2.5 slice.479
  203.2 1.6 copy-done
  204.8 46.0 %fusion.55 = f32[4,16,128,128]{3,2,1,0:T(8,128)} fusion(f32[4,1,16,128,128]{4,3,2,0,1:T(8,128)} %get-tuple-element.6, f32[4,1,16,128,128]{4,3,2,0,1:T(8,128)} %slice.479, f32[4,1,24,128,128]{4,3,2,0,1:T(8,128)} %copy-done, f32[16,128,128]{2,1,0:T(8,128)S(1)} %fusion.66, f32[128,128]{1,0:T(8,128)S(1)} %bitcast.47, f32[16,128,128]{2,1,0:T(8,128)S(1)} %bitcast.45, ...), kind=kLoop, calls=%fused_computation.102 | loop fusion | flops 47185920 | bytes 53542912 | tf_op jit(solution)/shard_map/reduce_sum | solution.py:96
  250.8 0.0 reduce-scatter.2.cloned.1.call-update
  250.9 54.3 %reduce-scatter.2.cloned.1.call-done = f32[4,16,64,128]{3,2,1,0:T(8,128)} async-done(((f32[4,16,128,128]{3,2,1,0:T(8,128)}), f32[4,16,64,128]{3,2,1,0:T(8,128)}) %reduce-scatter.2.cloned.1.call-update) | async-done | bytes 2097168 | tf_op jit(solution)/shard_map/reduce_scatter | solution.py:97
  305.2 3.2 %broadcast_multiply_fusion.1 = f32[4,16,64,128]{3,2,1,0:T(8,128)} fusion(f32[4,16,64,128]{3,2,1,0:T(8,128)} %reduce-scatter.2.cloned.1.call-done), kind=kLoop, calls=%fused_computation.183 | loop fusion | flops 524288 | bytes 4194304 | tf_op jit(solution)/shard_map/div | solution.py:98
  (14 shorter events, 0.1 us)
Async XLA Ops:
  6.5 12.6 %copy-start.5 = (f32[1,16,128,128]{3,2,1,0:T(8,128)S(1)}, f32[1,16,128,128]{3,2,1,0:T(8,128)}, u32[]{:S(2)}) copy-start(f32[1,16,128,128]{3,2,1,0:T(8,128)} %param.9) | copy-start | bytes 3145732
  6.5 12.9 %copy-start.4 = (f32[16,128,128]{2,1,0:T(8,128)S(1)}, f32[16,128,128]{2,1,0:T(8,128)}, u32[]{:S(2)}) copy-start(f32[16,128,128]{2,1,0:T(8,128)} %param.10) | copy-start | bytes 3145732
  6.5 60.3 %all-gather.2.cloned.1.call-start = ((), (), s32[]{:S(2)}) async-start(), calls=%async_computation.1 | async-start | bytes 6291456 | tf_op jit(solution)/shard_map/all_gather | solution.py:69
  7.3 297.9 %reduce-scatter.2.cloned.1.call-start = ((), (), s32[]{:S(2)}) async-start(), calls=%async_computation.2 | async-start | bytes 6291456 | tf_op jit(solution)/shard_map/reduce_scatter | solution.py:97
  8.4 11.0 %collective-permute-start = (f32[1,4,128,128]{3,2,1,0:T(8,128)S(1)}, f32[1,4,128,128]{3,2,1,0:T(8,128)S(1)}, u32[]{:S(2)}, u32[]{:S(2)}) collective-permute-start(f32[1,4,128,128]{3,2,1,0:T(8,128)S(1)} %get-tuple-element.15), channel_id=1, source_target_pairs={{1,0},{2,1},{3,2},{4,3},{5,4},{6,5},{7,6},{8,7},{9,8},{10,9},{11,1... | collective-permute-start | bytes 786440 | tf_op jit(solution)/shard_map/ppermute | solution.py:18
  11.0 8.1 %collective-permute-start.1 = (f32[1,4,128,128]{3,2,1,0:T(8,128)S(1)}, f32[1,4,128,128]{3,2,1,0:T(8,128)S(1)}, u32[]{:S(2)}, u32[]{:S(2)}) collective-permute-start(f32[1,4,128,128]{3,2,1,0:T(8,128)S(1)} %get-tuple-element.16), channel_id=1, source_target_pairs={{0,1},{1,2},{2,3},{3,4},{4,5},{5,6},{6,7},{7,8},{8,9},{9,10},{10,1... | collective-permute-start | bytes 786440 | tf_op jit(solution)/shard_map/ppermute | solution.py:15
  15.3 4.1 %copy-start.7 = (f32[1,16,128,128]{3,2,1,0:T(8,128)S(1)}, f32[1,16,128,128]{3,2,1,0:T(8,128)}, u32[]{:S(2)}) copy-start(f32[1,16,128,128]{3,2,1,0:T(8,128)} %param.8) | copy-start | bytes 3145732
  69.5 1.9 copy-start.3
  71.4 7.1 %copy-start.6 = (f32[1,16,128,128]{3,2,1,0:T(8,128)S(1)}, f32[1,16,128,128]{3,2,1,0:T(8,128)}, u32[]{:S(2)}) copy-start(f32[1,16,128,128]{3,2,1,0:T(8,128)} %get-tuple-element.7) | copy-start | bytes 3145732
  72.9 49.8 %collective-permute-start.2 = (f32[4,4,128,128]{3,2,1,0:T(8,128)}, f32[4,4,128,128]{3,2,1,0:T(8,128)}, u32[]{:S(2)}, u32[]{:S(2)}) collective-permute-start(f32[4,4,128,128]{3,2,1,0:T(8,128)} %get-tuple-element.11), channel_id=1, source_target_pairs={{0,1},{1,2},{2,3},{3,4},{4,5},{5,6},{6,7},{7,8},{8,9},{9,10},{10,1... | collective-permute-start | bytes 3145736 | tf_op jit(solution)/shard_map/ppermute | solution.py:15
  76.6 46.2 %collective-permute-start.3 = (f32[4,4,128,128]{3,2,1,0:T(8,128)}, f32[4,4,128,128]{3,2,1,0:T(8,128)}, u32[]{:S(2)}, u32[]{:S(2)}) collective-permute-start(f32[4,4,128,128]{3,2,1,0:T(8,128)} %get-tuple-element.12), channel_id=1, source_target_pairs={{1,0},{2,1},{3,2},{4,3},{5,4},{6,5},{7,6},{8,7},{9,8},{10,9},{11,1... | collective-permute-start | bytes 3145736 | tf_op jit(solution)/shard_map/ppermute | solution.py:18
  79.4 27.6 %collective-permute-start.4 = (f32[1,4,128,128]{3,2,1,0:T(8,128)}, f32[1,4,128,128]{3,2,1,0:T(8,128)S(1)}, u32[]{:S(2)}, u32[]{:S(2)}) collective-permute-start(f32[1,4,128,128]{3,2,1,0:T(8,128)} %get-tuple-element.13), channel_id=1, source_target_pairs={{1,0},{2,1},{3,2},{4,3},{5,4},{6,5},{7,6},{8,7},{9,8},{10,9},{11,1... | collective-permute-start | bytes 786440 | tf_op jit(solution)/shard_map/ppermute | solution.py:18
  82.8 24.1 %collective-permute-start.5 = (f32[1,4,128,128]{3,2,1,0:T(8,128)}, f32[1,4,128,128]{3,2,1,0:T(8,128)}, u32[]{:S(2)}, u32[]{:S(2)}) collective-permute-start(f32[1,4,128,128]{3,2,1,0:T(8,128)} %get-tuple-element.14), channel_id=1, source_target_pairs={{0,1},{1,2},{2,3},{3,4},{4,5},{5,6},{6,7},{7,8},{8,9},{9,10},{10,1... | collective-permute-start | bytes 786440 | tf_op jit(solution)/shard_map/ppermute | solution.py:15
  125.9 3.9 %copy-start.1 = (f32[4,1,24,128,128]{4,3,2,0,1:T(8,128)}, f32[4,1,24,128,128]{4,3,2,0,1:T(8,128)S(1)}, u32[]{:S(2)}) copy-start(f32[4,1,24,128,128]{4,3,2,0,1:T(8,128)S(1)} %maximum_bitcast_fusion) | copy-start | bytes 18874372
  172.1 27.8 %copy-start.2 = (f32[4,16,128,128]{3,2,1,0:T(8,128)S(1)}, f32[4,16,128,128]{3,2,1,0:T(8,128)}, u32[]{:S(2)}) copy-start(f32[4,16,128,128]{3,2,1,0:T(8,128)} %get-tuple-element.5) | copy-start | bytes 12582916
  173.9 26.0 %collective-permute-start.6 = (f32[4,4,128,128]{3,2,1,0:T(8,128)S(1)}, f32[4,4,128,128]{3,2,1,0:T(8,128)S(1)}, u32[]{:S(2)}, u32[]{:S(2)}) collective-permute-start(f32[4,4,128,128]{3,2,1,0:T(8,128)S(1)} %get-tuple-element.9), channel_id=1, source_target_pairs={{0,1},{1,2},{2,3},{3,4},{4,5},{5,6},{6,7},{7,8},{8,9},{9,10},{10,1... | collective-permute-start | bytes 3145736 | tf_op jit(solution)/shard_map/ppermute | solution.py:15
  177.0 23.0 %collective-permute-start.7 = (f32[4,4,128,128]{3,2,1,0:T(8,128)S(1)}, f32[4,4,128,128]{3,2,1,0:T(8,128)S(1)}, u32[]{:S(2)}, u32[]{:S(2)}) collective-permute-start(f32[4,4,128,128]{3,2,1,0:T(8,128)S(1)} %get-tuple-element.10), channel_id=1, source_target_pairs={{1,0},{2,1},{3,2},{4,3},{5,4},{6,5},{7,6},{8,7},{9,8},{10,9},{11,1... | collective-permute-start | bytes 3145736 | tf_op jit(solution)/shard_map/ppermute | solution.py:18
  200.7 4.1 %copy-start = (f32[4,1,24,128,128]{4,3,2,0,1:T(8,128)}, f32[4,1,24,128,128]{4,3,2,0,1:T(8,128)S(1)}, u32[]{:S(2)}) copy-start(f32[4,1,24,128,128]{4,3,2,0,1:T(8,128)S(1)} %maximum_bitcast_fusion.1) | copy-start | bytes 18874372
Sparse Core Ops, SparseCore 0:
  8.9 57.8 all-gather.1
  251.0 54.1 reduce-scatter.1
where the time goes:
time: 317 us; the launch traced here: 315 us
  waiting for transfers between devices  141 us (44%)
  other arithmetic  122 us (38%)
  starting transfers between devices  21.9 us (7%)
  between operations  15.7 us (5%)
  local copies, waits for them, and re-layouts  15.5 us (5%)
    reduce_scatter x1, waiting for transfers between devices, per_device(): lax.psum_scatter(local_sum, 'shot', scatter_dimension=2, tiled=True)  54.3 us
    reduce_sum x1, other arithmetic, per_device(): jnp.sum(born_zero[None] * early_field + born_one[None] * late_field, axis=1)  46 us
    all_gather x1, waiting for transfers between devices, per_device(): probes = lax.all_gather(probe_panel, 'shot', axis=2, tiled=True)  43.8 us
    reshape x1, other arithmetic, per_device(): weighted.reshape(probe_count * shot_count, count_z, width_x, width_y)  42.2 us
    ppermute x4, waiting for transfers between devices, extended(): lax.ppermute(lax.slice_in_dim(block, block.shape[dim] - width, None, axis...  23.2 us
    ppermute x4, waiting for transfers between devices, extended(): lax.ppermute(lax.slice_in_dim(block, 0, width, axis=dim), axis, backward)  18.7 us
    mul x1, other arithmetic, per_device(): probes[:, None] * born_one[None]  15.7 us
    ppermute x4, starting transfers between devices, extended(): lax.ppermute(lax.slice_in_dim(block, block.shape[dim] - width, None, axis...  11.8 us
  transfers between devices with their start and end apart: 10, of which 5 were waited for; matrix products, arithmetic and copies ran while one was open for 8% of the time, Pallas kernels for 0%

commit v1 on v0

v1 whole, which is shorter than its diff:
```python
import functools

import jax
import jax.numpy as jnp
from jax import lax
from jax.experimental import pallas as pl
from jax.experimental.pallas import tpu as pltpu
from jax.sharding import PartitionSpec as P

CENTER = -205.0 / 72.0
WEIGHTS = (8.0 / 5.0, -1.0 / 5.0, 8.0 / 315.0, -1.0 / 560.0)
SCALED = (8064.0, -1008.0, 128.0, -9.0)
REACH = 4
EDGE = 8
MESH = pl.DeviceIdType.MESH


def kernel(
    shots,
    slabs,
    prev_ref,
    now_ref,
    vel_ref,
    probe_ref,
    depth_ref,
    column_ref,
    strength_ref,
    wells_ref,
    out_ref,
    now,
    prev,
    vel,
    velq,
    upc,
    bz,
    b1,
    bzq,
    b1q,
    cnt,
    cntq,
    pe,
    f,
    w,
    accz,
    accx,
    gotz,
    gotx,
    band,
    loc_sem,
    now_s,
    now_r,
    upc_s,
    upc_r,
    bzh_s,
    bzh_r,
    pz_s,
    pz_r,
    px_s,
    px_r,
    bzq_s,
    bzq_r,
    b1q_s,
    b1q_r,
    cnt_s,
    cnt_r,
    cz_s,
    cz_r,
    cx_s,
    cx_r,
):
    me = lax.axis_index("shot")
    slab = lax.axis_index("space")
    nz, nx, ny = vel_ref.shape
    probes, _, xw, _ = probe_ref.shape
    chunks = nz // REACH
    has_lo, has_hi = slab > 0, slab < slabs - 1
    has_left, has_right = me > 0, me < shots - 1
    lo, hi = jnp.maximum(slab - 1, 0), jnp.minimum(slab + 1, slabs - 1)
    left, right = jnp.maximum(me - 1, 0), jnp.minimum(me + 1, shots - 1)

    def remote(src, dst, ss, rs, dev):
        return pltpu.make_async_remote_copy(
            src_ref=src, dst_ref=dst, send_sem=ss, recv_sem=rs, device_id=dev, device_id_type=MESH
        )

    class Pair:
        def __init__(self, down, up, low, high):
            self.down, self.up, self.low, self.high = down, up, low, high

        def start(self):
            pl.when(self.low)(self.down.start)
            pl.when(self.high)(self.up.start)

        def wait_recv(self):
            pl.when(self.low)(self.up.wait_recv)
            pl.when(self.high)(self.down.wait_recv)

        def wait_send(self):
            pl.when(self.low)(self.down.wait_send)
            pl.when(self.high)(self.up.wait_send)

    def zpair(src_lo, src_hi, dst_lo, dst_hi, ss0, ss1, rs0, rs1):
        return Pair(
            remote(src_lo, dst_hi, ss0, rs1, (me, lo)),
            remote(src_hi, dst_lo, ss1, rs0, (me, hi)),
            has_lo,
            has_hi,
        )

    def xpair(src_lo, src_hi, dst_lo, dst_hi, ss0, ss1, rs0, rs1):
        return Pair(
            remote(src_lo, dst_hi, ss0, rs1, (left, slab)),
            remote(src_hi, dst_lo, ss1, rs0, (right, slab)),
            has_left,
            has_right,
        )

    barrier = pltpu.get_barrier_semaphore()

    def greet(dev):
        pl.semaphore_signal(barrier, inc=1, device_id=dev, device_id_type=MESH)

    pl.when(has_lo)(lambda: greet((me, lo)))
    pl.when(has_hi)(lambda: greet((me, hi)))
    for step in range(1, shots):
        greet((lax.rem(me + step, shots), slab))

    inner = pl.ds(EDGE, nx)
    mine = pl.ds(REACH, nz)
    top = pl.ds(0, REACH)
    bottom = pl.ds(REACH + nz, REACH)
    first_x = pl.multiple_of(me * xw, 8)
    rows = pl.ds(EDGE, xw)
    loads = [
        pltpu.make_async_copy(now_ref.at[0], now.at[mine, inner], loc_sem.at[0]),
        pltpu.make_async_copy(vel_ref, vel, loc_sem.at[1]),
        pltpu.make_async_copy(prev_ref.at[0], prev, loc_sem.at[2]),
        pltpu.make_async_copy(vel_ref.at[:, pl.ds(first_x, xw)], velq, loc_sem.at[3]),
        pltpu.make_async_copy(probe_ref, pe.at[:, mine, rows], loc_sem.at[4]),
    ]
    for load in loads:
        load.start()

    for ref in (now, upc, bz):
        ref[:, pl.ds(0, EDGE)] = jnp.zeros((nz + 2 * REACH, EDGE, ny), jnp.float32)
        ref[:, pl.ds(EDGE + nx, EDGE)] = jnp.zeros((nz + 2 * REACH, EDGE, ny), jnp.float32)

    def clear_end(place):
        for ref in (now, upc, bz):
            ref[place, inner] = jnp.zeros((REACH, nx, ny), jnp.float32)
        for p in range(probes):
            pe[p, place, rows] = jnp.zeros((REACH, xw, ny), jnp.float32)

    def clear_side(place):
        for p in range(probes):
            pe[p, mine, place] = jnp.zeros((nz, EDGE, ny), jnp.float32)

    pl.when(jnp.logical_not(has_lo))(lambda: clear_end(top))
    pl.when(jnp.logical_not(has_hi))(lambda: clear_end(bottom))
    pl.when(jnp.logical_not(has_left))(lambda: clear_side(pl.ds(0, EDGE)))
    pl.when(jnp.logical_not(has_right))(lambda: clear_side(pl.ds(EDGE + xw, EDGE)))
    w[pl.ds(0, REACH)] = jnp.zeros((REACH, xw + 4 * EDGE, ny), jnp.float32)
    w[pl.ds(REACH + nz, REACH)] = jnp.zeros((REACH, xw + 4 * EDGE, ny), jnp.float32)
    w[mine, pl.ds(0, 2 * EDGE)] = jnp.zeros((nz, 2 * EDGE, ny), jnp.float32)
    w[mine, pl.ds(2 * EDGE + xw, 2 * EDGE)] = jnp.zeros((nz, 2 * EDGE, ny), jnp.float32)

    arrivals = (
        shots - 1 + has_lo.astype(jnp.int32) + has_hi.astype(jnp.int32)
    )
    pl.semaphore_wait(barrier, arrivals)

    now_pair = zpair(
        now_ref.at[0, pl.ds(0, REACH)],
        now_ref.at[0, pl.ds(nz - REACH, REACH)],
        now.at[top, inner],
        now.at[bottom, inner],
        now_s.at[0], now_s.at[1], now_r.at[0], now_r.at[1],
    )
    now_pair.start()
    px_pair = xpair(
        probe_ref.at[:, :, pl.ds(0, EDGE)],
        probe_ref.at[:, :, pl.ds(xw - EDGE, EDGE)],
        pe.at[:, mine, pl.ds(0, EDGE)],
        pe.at[:, mine, pl.ds(EDGE + xw, EDGE)],
        px_s.at[0], px_s.at[1], px_r.at[0], px_r.at[1],
    )
    px_pair.start()
    pz_pair = zpair(
        probe_ref.at[:, pl.ds(0, REACH)],
        probe_ref.at[:, pl.ds(nz - REACH, REACH)],
        pe.at[:, top, rows],
        pe.at[:, bottom, rows],
        pz_s.at[0], pz_s.at[1], pz_r.at[0], pz_r.at[1],
    )
    pz_pair.start()

    row_id = lax.broadcasted_iota(jnp.int32, (ny, ny), 0)
    col_id = lax.broadcasted_iota(jnp.int32, (ny, ny), 1)
    apart = jnp.abs(row_id - col_id)
    half = jnp.zeros((ny, ny), jnp.float32)
    for k in range(1, REACH + 1):
        half = jnp.where(apart == k, SCALED[k - 1], half)
    half = half.astype(jnp.bfloat16)
    band[pl.ds(0, ny)] = half
    band[pl.ds(ny, ny)] = half

    wells = wells_ref[...]
    count = wells.shape[1]
    hot_x = (lax.broadcasted_iota(jnp.int32, (nx, count), 0) == lax.div(wells, ny)).astype(jnp.float32)
    hot_y = (lax.broadcasted_iota(jnp.int32, (ny, count), 0) == lax.rem(wells, ny)).astype(jnp.float32)
    cnt[...] = lax.dot_general(
        hot_x.astype(jnp.bfloat16),
        hot_y.astype(jnp.bfloat16),
        (((1,), (1,)), ((), ())),
        preferred_element_type=jnp.float32,
    )

    def partner_copy(step, kind):
        other = lax.rem(me + step, shots)
        source = lax.rem(me - step + shots, shots)
        start_x = pl.multiple_of(other * xw, 8)
        if kind == "cnt":
            return remote(cnt.at[pl.ds(start_x, xw)], cntq.at[me], cnt_s.at[other], cnt_r.at[me], (other, slab))
        if kind == "b1":
            return remote(
                b1.at[:, pl.ds(start_x, xw)], b1q.at[me], b1q_s.at[other], b1q_r.at[me], (other, slab)
            )
        place = {"bz": mine, "top": top, "bottom": bottom}[kind]
        index = {"bz": 0, "top": 1, "bottom": 2}[kind]
        return remote(
            bz.at[place, pl.ds(start_x, xw + 2 * EDGE)],
            bzq.at[me, place],
            bzq_s.at[other, index],
            bzq_r.at[me, index],
            (other, slab),
        )

    def send(kind):
        for step in range(1, shots):
            partner_copy(step, kind).start()

    send("cnt")
    cntq[me] = cnt[pl.ds(first_x, xw)]

    def laplace(ref, z, first, count):
        here = pl.ds(first, count)
        middle = ref[pl.ds(z, REACH), here]
        flat = middle.reshape(REACH * count, ny)
        high = flat.astype(jnp.bfloat16)
        low = (flat - high.astype(jnp.float32)).astype(jnp.bfloat16)
        along = jnp.dot(
            jnp.concatenate([high, low], axis=1), band[...], preferred_element_type=jnp.float32
        ).reshape(REACH, count, ny)
        total = (3.0 * CENTER) * middle + (1.0 / 5040.0) * along
        for k in range(1, REACH + 1):
            near = (
                ref[pl.ds(z + k, REACH), here]
                + ref[pl.ds(z - k, REACH), here]
                + ref[pl.ds(z, REACH), pl.ds(first + k, count)]
                + ref[pl.ds(z, REACH), pl.ds(first - k, count)]
            )
            total = total + WEIGHTS[k - 1] * near
        return total

    src_depth, src_column, src_strength = depth_ref[0], column_ref[0], strength_ref[0]
    xpart = min(64, nx)
    layer_id = lax.broadcasted_iota(jnp.int32, (REACH, xpart, ny), 0)
    cell_id = lax.broadcasted_iota(jnp.int32, (REACH, xpart, ny), 1) * ny + lax.broadcasted_iota(
        jnp.int32, (REACH, xpart, ny), 2
    )

    def step_zero(c):
        z = c * REACH
        for x0 in range(0, nx, xpart):
            xs = pl.ds(x0, xpart)
            xe = pl.ds(EDGE + x0, xpart)
            zs = pl.ds(z, REACH)
            ze = pl.ds(REACH + z, REACH)
            field = vel[zs, xs] * laplace(now, REACH + z, EDGE + x0, xpart)
            bz[ze, xe] = field
            hit = (layer_id + (slab * nz + z) == src_depth) & (cell_id + x0 * ny == src_column)
            upc[ze, xe] = (
                2.0 * now[ze, xe] - prev[zs, xs] + field + jnp.where(hit, src_strength, 0.0)
            )

    def step_one(c):
        z = c * REACH
        for x0 in range(0, nx, xpart):
            xs = pl.ds(x0, xpart)
            b1[pl.ds(z, REACH), xs] = vel[pl.ds(z, REACH), xs] * laplace(
                upc, REACH + z, EDGE + x0, xpart
            )

    def over(body, begin, end):
        def run(c, carry):
            body(c)
            return carry

        lax.fori_loop(begin, end, run, 0)

    loads[0].wait()
    loads[1].wait()
    loads[2].wait()
    over(step_zero, 1, chunks - 1)
    now_pair.wait_recv()

    def ends(body):
        over(lambda i: body(i * (chunks - 1)), 0, 2)

    ends(step_zero)

    def halo(ref, ss, rs):
        return zpair(
            ref.at[pl.ds(REACH, REACH), inner],
            ref.at[pl.ds(nz, REACH), inner],
            ref.at[top, inner],
            ref.at[bottom, inner],
            ss.at[0], ss.at[1], rs.at[0], rs.at[1],
        )

    upc_pair = halo(upc, upc_s, upc_r)
    upc_pair.start()
    bzh_pair = halo(bz, bzh_s, bzh_r)
    bzh_pair.start()
    send("bz")
    over(step_one, 1, chunks - 1)
    upc_pair.wait_recv()
    ends(step_one)
    send("b1")
    bzh_pair.wait_recv()
    send("top")
    send("bottom")
    own_bz = pltpu.make_async_copy(
        bz.at[:, pl.ds(first_x, xw + 2 * EDGE)], bzq.at[me], loc_sem.at[5]
    )
    own_b1 = pltpu.make_async_copy(b1.at[:, pl.ds(first_x, xw)], b1q.at[me], loc_sem.at[6])
    own_bz.start()
    own_b1.start()
    loads[3].wait()
    loads[4].wait()
    px_pair.wait_recv()
    pz_pair.wait_recv()
    own_bz.wait()
    own_b1.wait()

    def cz_pair(p):
        return zpair(
            accz.at[0, p], accz.at[1, p], gotz.at[0, p], gotz.at[1, p],
            cz_s.at[0, p], cz_s.at[1, p], cz_r.at[0, p], cz_r.at[1, p],
        )

    def cx_pair(p):
        return xpair(
            accx.at[0, p], accx.at[1, p], gotx.at[0, p], gotx.at[1, p],
            cx_s.at[0, p], cx_s.at[1, p], cx_r.at[0, p], cx_r.at[1, p],
        )

    wide = pl.ds(2 * EDGE, xw)

    def each_shot(t):
        shot = lax.rem(me + t, shots)

        @pl.when(t > 0)
        def _():
            start_x = pl.multiple_of(me * xw, 8)
            whole_x = pl.ds(start_x, xw + 2 * EDGE)
            for index, place in enumerate((mine, top, bottom)):
                remote(
                    bz.at[place, whole_x], bzq.at[shot, place],
                    bzq_s.at[shot, index], bzq_r.at[shot, index], (shot, slab),
                ).wait_recv()
            remote(
                b1.at[:, pl.ds(start_x, xw)], b1q.at[shot],
                b1q_s.at[shot], b1q_r.at[shot], (shot, slab),
            ).wait_recv()
            remote(
                cnt.at[pl.ds(start_x, xw)], cntq.at[shot], cnt_s.at[shot], cnt_r.at[shot], (shot, slab)
            ).wait_recv()

        def each_probe(p):
            @pl.when(t == 0)
            def _():
                out_ref[p] = jnp.zeros((nz, xw, ny), jnp.float32)
                for side in range(2):
                    accz[side, p] = jnp.zeros((REACH, xw, ny), jnp.float32)
                    accx[side, p] = jnp.zeros((nz, EDGE, ny), jnp.float32)

            f[top, rows] = pe[p, top, rows] * bzq[shot, top, rows]
            f[bottom, rows] = pe[p, bottom, rows] * bzq[shot, bottom, rows]

            def make_first(c):
                ze = pl.ds(REACH + c * REACH, REACH)
                f[ze] = pe[p, ze] * bzq[shot, ze]

            over(make_first, 0, chunks)

            def forward(c):
                z = c * REACH
                zs = pl.ds(z, REACH)
                ze = pl.ds(REACH + z, REACH)
                lap = laplace(f, REACH + z, EDGE, xw)
                first = f[ze, rows]
                v = velq[zs]
                one = b1q[shot, zs]
                tally = cntq[shot][None]
                second = 2.0 * first + v * lap + pe[p, ze, rows] * one
                late = tally * second
                w[ze, wide] = v * late
                out_ref[p, zs] += bzq[shot, ze, rows] * (tally * first + 2.0 * late) + one * late

            over(forward, 0, chunks)

            def adjoint(c):
                z = c * REACH
                zs = pl.ds(z, REACH)
                ze = pl.ds(REACH + z, REACH)
                out_ref[p, zs] += bzq[shot, ze, rows] * laplace(w, REACH + z, 2 * EDGE, xw)
                left_sum = jnp.zeros((REACH, EDGE, ny), jnp.float32)
                right_sum = jnp.zeros((REACH, EDGE, ny), jnp.float32)
                for k in range(1, REACH + 1):
                    left_sum += WEIGHTS[k - 1] * w[ze, pl.ds(EDGE + k, EDGE)]
                    right_sum += WEIGHTS[k - 1] * w[ze, pl.ds(2 * EDGE + xw - k, EDGE)]
                accx[0, p, zs] += bzq[shot, ze, pl.ds(0, EDGE)] * left_sum
                accx[1, p, zs] += bzq[shot, ze, pl.ds(EDGE + xw, EDGE)] * right_sum

            for j in range(1, REACH + 1):
                low_sum = jnp.zeros((xw, ny), jnp.float32)
                high_sum = jnp.zeros((xw, ny), jnp.float32)
                for k in range(j, REACH + 1):
                    low_sum += WEIGHTS[k - 1] * w[REACH + k - j, wide]
                    high_sum += WEIGHTS[k - 1] * w[REACH + nz - 1 - (k - j), wide]
                accz[0, p, REACH - j] += bzq[shot, REACH - j, rows] * low_sum
                accz[1, p, j - 1] += bzq[shot, REACH + nz + j - 1, rows] * high_sum
            pl.when(t == shots - 1)(lambda: cz_pair(p).start())
            over(adjoint, 0, chunks)
            pl.when(t == shots - 1)(lambda: cx_pair(p).start())

        over(each_probe, 0, probes)

    over(each_shot, 0, shots)

    scale = 1.0 / shots

    def finish(p):
        cz_pair(p).wait_recv()
        cx_pair(p).wait_recv()

        @pl.when(has_lo)
        def _():
            out_ref[p, pl.ds(0, REACH)] += gotz[0, p]

        @pl.when(has_hi)
        def _():
            out_ref[p, pl.ds(nz - REACH, REACH)] += gotz[1, p]

        @pl.when(has_left)
        def _():
            out_ref[p, :, pl.ds(0, EDGE)] += gotx[0, p]

        @pl.when(has_right)
        def _():
            out_ref[p, :, pl.ds(xw - EDGE, EDGE)] += gotx[1, p]

        out_ref[p] = out_ref[p] * scale
        cz_pair(p).wait_send()
        cx_pair(p).wait_send()

    over(finish, 0, probes)
    for pair in (now_pair, px_pair, pz_pair, upc_pair, bzh_pair):
        pair.wait_send()
    for kind in ("cnt", "bz", "b1", "top", "bottom"):
        for step in range(1, shots):
            partner_copy(step, kind).wait_send()


def per_device(shots, slabs, *arrays):
    nz, nx, ny = arrays[2].shape
    probes, _, xw, _ = arrays[3].shape
    tall = nz + 2 * REACH
    f32 = jnp.float32
    dma = pltpu.SemaphoreType.DMA
    two = [dma((2,))] * 2
    anywhere = pl.BlockSpec(memory_space=pl.ANY)
    scalar = pl.BlockSpec(memory_space=pltpu.SMEM)
    vector = pl.BlockSpec(memory_space=pltpu.VMEM)
    return pl.pallas_call(
        functools.partial(kernel, shots, slabs),
        out_shape=jax.ShapeDtypeStruct((probes, nz, xw, ny), f32),
        in_specs=[anywhere] * 4 + [scalar] * 3 + [vector],
        out_specs=vector,
        scratch_shapes=[
            pltpu.VMEM((tall, nx + 2 * EDGE, ny), f32),
            pltpu.VMEM((nz, nx, ny), f32),
            pltpu.VMEM((nz, nx, ny), f32),
            pltpu.VMEM((nz, xw, ny), f32),
            pltpu.VMEM((tall, nx + 2 * EDGE, ny), f32),
            pltpu.VMEM((tall, nx + 2 * EDGE, ny), f32),
            pltpu.VMEM((nz, nx, ny), f32),
            pltpu.VMEM((shots, tall, xw + 2 * EDGE, ny), f32),
            pltpu.VMEM((shots, nz, xw, ny), f32),
            pltpu.VMEM((nx, ny), f32),
            pltpu.VMEM((shots, xw, ny), f32),
            pltpu.VMEM((probes, tall, xw + 2 * EDGE, ny), f32),
            pltpu.VMEM((tall, xw + 2 * EDGE, ny), f32),
            pltpu.VMEM((tall, xw + 4 * EDGE, ny), f32),
            pltpu.VMEM((2, probes, REACH, xw, ny), f32),
            pltpu.VMEM((2, probes, nz, EDGE, ny), f32),
            pltpu.VMEM((2, probes, REACH, xw, ny), f32),
            pltpu.VMEM((2, probes, nz, EDGE, ny), f32),
            pltpu.VMEM((2 * ny, ny), jnp.bfloat16),
            dma((7,)),
            *two,
            *two,
            *two,
            *two,
            *two,
            dma((shots, 3)),
            dma((shots, 3)),
            dma((shots,)),
            dma((shots,)),
            dma((shots,)),
            dma((shots,)),
            dma((2, probes)),
            dma((2, probes)),
            dma((2, probes)),
            dma((2, probes)),
        ],
        compiler_params=pltpu.CompilerParams(
            collective_id=0, has_side_effects=True, vmem_limit_bytes=48 * 1024 * 1024
        ),
    )(*arrays)


def solution(mesh):
    return jax.shard_map(
        functools.partial(per_device, mesh.shape["shot"], mesh.shape["space"]),
        mesh=mesh,
        in_specs=(
            P("shot", "space", None, None),
            P("shot", "space", None, None),
            P("space", None, None),
            P(None, "space", "shot", None),
            P("shot"),
            P("shot"),
            P("shot"),
            P("shot", None),
        ),
        out_specs=P(None, "space", "shot", None),
        check_vma=False,
    )
```

time: 317 us -> 72.2 us (0.23)
  waiting for transfers between devices: 141 us -> 0 us
  other arithmetic: 122 us -> 0 us
  Pallas kernels: 0 us -> 63.4 us
  starting transfers between devices: 21.9 us -> 0 us
  between operations: 15.7 us -> 1.96 us
  local copies, waits for them, and re-layouts: 15.5 us -> 5.67 us
    pallas_call x0 -> x1, Pallas kernels: none -> 63.4 us  [per_device(): pl.pallas_call(functools.partial(kernel, shots, slabs), out_shape=jax.Sha...]
    reduce_scatter x1 -> x0, waiting for transfers between devices: 54.3 us -> none  [per_device(): lax.psum_scatter(local_sum, 'shot', scatter_dimension=2, tiled=True)]
    reshape x3 -> x0, other arithmetic: 46.2 us -> none  [the longest x1 42.2 us: per_device(): weighted.reshape(probe_count * shot_count, count_z, width_x, width_y)]
    reduce_sum x1 -> x0, other arithmetic: 46 us -> none  [per_device(): jnp.sum(born_zero[None] * early_field + born_one[None] * late_field, axis=1)]
    all_gather x1 -> x0, waiting for transfers between devices: 43.8 us -> none  [per_device(): probes = lax.all_gather(probe_panel, 'shot', axis=2, tiled=True)]
    ppermute x8 -> x0, waiting for transfers between devices: 41.8 us -> none  [the longest x4 23.2 us: extended(): lax.ppermute(lax.slice_in_dim(block, block.shape[dim] - width, None, axis...]
    ppermute x8 -> x0, starting transfers between devices: 21.8 us -> none  [the longest x4 11.8 us: extended(): lax.ppermute(lax.slice_in_dim(block, block.shape[dim] - width, None, axis...]
    mul x2 -> x0, other arithmetic: 18.3 us -> none  [the longest x1 15.7 us: per_device(): probes[:, None] * born_one[None]]
  transfers between devices with their start and end apart: 10 -> 0, of which waited for: 5 -> 0; matrix products, arithmetic and copies ran while one was open for 8% -> 0% of each run, Pallas kernels for 0% -> 0%
where the time goes in v1:
time: 72.2 us; the launch traced here: 71.1 us
  Pallas kernels  63.4 us (88%)
  local copies, waits for them, and re-layouts  5.67 us (8%)
  between operations  1.96 us (3%)
    pallas_call x1, Pallas kernels, per_device(): pl.pallas_call(functools.partial(kernel, shots, slabs), out_shape=jax.Sha...  63.4 us
    unnamed x9, local copies, waits for them, and re-layouts  5.67 us

profile of v1, /device:TPU:9, one launch (start us, length us, event | category | flops | bytes accessed | tf_op | source)
XLA Modules:
  0.0 71.1 jit_solution(9493733966706211709)
XLA Ops:
  1.9 0.0 copy-start
  2.0 1.2 %copy-done = f32[1,16,128,128]{3,2,1,0:T(8,128)S(1)} copy-done((f32[1,16,128,128]{3,2,1,0:T(8,128)S(1)}, f32[1,16,128,128]{3,2,1,0:T(8,128)}, u32[]{:S(2)}) %copy-start) | copy-done | bytes 1048600
  3.2 0.0 copy-start.1
  3.2 1.2 %copy-done.1 = f32[1,16,128,128]{3,2,1,0:T(8,128)S(1)} copy-done((f32[1,16,128,128]{3,2,1,0:T(8,128)S(1)}, f32[1,16,128,128]{3,2,1,0:T(8,128)}, u32[]{:S(2)}) %copy-start.1) | copy-done | bytes 1048600
  4.4 0.0 copy-start.2
  4.4 1.2 %copy-done.2 = f32[16,128,128]{2,1,0:T(8,128)S(1)} copy-done((f32[16,128,128]{2,1,0:T(8,128)S(1)}, f32[16,128,128]{2,1,0:T(8,128)}, u32[]{:S(2)}) %copy-start.2) | copy-done | bytes 1048600
  5.6 0.0 copy-start.3
  5.6 0.7 copy-done.3
  6.3 63.4 %shard_map.82 = f32[4,16,64,128]{3,2,1,0:T(8,128)S(1)} custom-call(f32[1,16,128,128]{3,2,1,0:T(8,128)S(1)} %copy-done, f32[1,16,128,128]{3,2,1,0:T(8,128)S(1)} %copy-done.1, f32[16,128,128]{2,1,0:T(8,128)S(1)} %copy-done.2, f32[4,16,64,128]{3,2,1,0:T(8,128)} %probe_ref.1, s32[1]{0:T(128)S(6)} %copy.10.depth_ref, s32[1]{0:T(128)S(6)} %copy.11.column_ref, ...), custom_call_target="tpu_custom_call" | custom-call | tf_op jit(solution)/shard_map/pallas_call | solution.py:486
  69.7 1.3 %copy.13 = f32[4,16,64,128]{3,2,1,0:T(8,128)} copy(f32[4,16,64,128]{3,2,1,0:T(8,128)S(1)} %shard_map.82) | data formatting | bytes 4194304
Async XLA Ops:
  1.9 1.2 %copy-start = (f32[1,16,128,128]{3,2,1,0:T(8,128)S(1)}, f32[1,16,128,128]{3,2,1,0:T(8,128)}, u32[]{:S(2)}) copy-start(f32[1,16,128,128]{3,2,1,0:T(8,128)} %prev_ref.1) | copy-start | bytes 3145732
  3.2 1.2 %copy-start.1 = (f32[1,16,128,128]{3,2,1,0:T(8,128)S(1)}, f32[1,16,128,128]{3,2,1,0:T(8,128)}, u32[]{:S(2)}) copy-start(f32[1,16,128,128]{3,2,1,0:T(8,128)} %now_ref.1) | copy-start | bytes 3145732
  4.4 1.2 %copy-start.2 = (f32[16,128,128]{2,1,0:T(8,128)S(1)}, f32[16,128,128]{2,1,0:T(8,128)}, u32[]{:S(2)}) copy-start(f32[16,128,128]{2,1,0:T(8,128)} %vel_ref.1) | copy-start | bytes 3145732
  5.6 0.7 copy-start.3

commit v2 on v1

--- a/solution.py
+++ b/solution.py
@@ -45,6 +45,8 @@
     accx,
     gotz,
     gotx,
+    sendpx,
+    gotpx,
     band,
     loc_sem,
     now_s,
@@ -154,6 +156,8 @@
     def clear_side(place):
         for p in range(probes):
             pe[p, mine, place] = jnp.zeros((nz, EDGE, ny), jnp.float32)
+        for shot in range(shots):
+            bzq[shot, mine, place] = jnp.zeros((nz, EDGE, ny), jnp.float32)
 
     pl.when(jnp.logical_not(has_lo))(lambda: clear_end(top))
     pl.when(jnp.logical_not(has_hi))(lambda: clear_end(bottom))
@@ -177,22 +181,30 @@
         now_s.at[0], now_s.at[1], now_r.at[0], now_r.at[1],
     )
     now_pair.start()
+
+    def pz_pair(p):
+        return zpair(
+            probe_ref.at[p, pl.ds(0, REACH)],
+            probe_ref.at[p, pl.ds(nz - REACH, REACH)],
+            pe.at[p, top, rows],
+            pe.at[p, bottom, rows],
+            pz_s.at[0, p], pz_s.at[1, p], pz_r.at[0, p], pz_r.at[1, p],
+        )
+
+
+    pair_z = nz // 2
+    loads[4].wait()
+    for p in range(probes):
+        for part in range(2):
+            zs = pl.ds(REACH + part * pair_z, pair_z)
+            into = pl.ds(part * REACH, REACH)
+            sendpx[0, p, :, into] = pe[p, zs, pl.ds(EDGE, REACH)]
+            sendpx[1, p, :, into] = pe[p, zs, pl.ds(EDGE + xw - REACH, REACH)]
     px_pair = xpair(
-        probe_ref.at[:, :, pl.ds(0, EDGE)],
-        probe_ref.at[:, :, pl.ds(xw - EDGE, EDGE)],
-        pe.at[:, mine, pl.ds(0, EDGE)],
-        pe.at[:, mine, pl.ds(EDGE + xw, EDGE)],
+        sendpx.at[0], sendpx.at[1], gotpx.at[0], gotpx.at[1],
         px_s.at[0], px_s.at[1], px_r.at[0], px_r.at[1],
     )
     px_pair.start()
-    pz_pair = zpair(
-        probe_ref.at[:, pl.ds(0, REACH)],
-        probe_ref.at[:, pl.ds(nz - REACH, REACH)],
-        pe.at[:, top, rows],
-        pe.at[:, bottom, rows],
-        pz_s.at[0], pz_s.at[1], pz_r.at[0], pz_r.at[1],
-    )
-    pz_pair.start()
 
     row_id = lax.broadcasted_iota(jnp.int32, (ny, ny), 0)
     col_id = lax.broadcasted_iota(jnp.int32, (ny, ny), 1)
@@ -215,29 +227,68 @@
         preferred_element_type=jnp.float32,
     )
 
+    ZERO = {
+        "bz": (0, pl.ds(2 * REACH, nz - 2 * REACH)),
+        "top": (1, top),
+        "bottom": (2, bottom),
+        "left": (3, mine),
+        "right": (4, mine),
+        "bz_low": (5, pl.ds(REACH, REACH)),
+        "bz_high": (6, pl.ds(nz, REACH)),
+    }
+    ONE = {
+        "b1": (0, pl.ds(REACH, nz - 2 * REACH)),
+        "b1_low": (1, pl.ds(0, REACH)),
+        "b1_high": (2, pl.ds(nz - REACH, REACH)),
+    }
+
     def partner_copy(step, kind):
         other = lax.rem(me + step, shots)
         source = lax.rem(me - step + shots, shots)
         start_x = pl.multiple_of(other * xw, 8)
         if kind == "cnt":
             return remote(cnt.at[pl.ds(start_x, xw)], cntq.at[me], cnt_s.at[other], cnt_r.at[me], (other, slab))
-        if kind == "b1":
+        if kind in ONE:
+            index, place = ONE[kind]
             return remote(
-                b1.at[:, pl.ds(start_x, xw)], b1q.at[me], b1q_s.at[other], b1q_r.at[me], (other, slab)
+                b1.at[place, pl.ds(start_x, xw)],
+                b1q.at[me, place],
+                b1q_s.at[other, index],
+                b1q_r.at[me, index],
+                (other, slab),
             )
-        place = {"bz": mine, "top": top, "bottom": bottom}[kind]
-        index = {"bz": 0, "top": 1, "bottom": 2}[kind]
+        index, place = ZERO[kind]
+        if kind == "left":
+            from_x, to_x = pl.ds(start_x, EDGE), pl.ds(0, EDGE)
+        elif kind == "right":
+            from_x, to_x = pl.ds(pl.multiple_of(start_x + EDGE + xw, 8), EDGE), pl.ds(EDGE + xw, EDGE)
+        else:
+            from_x, to_x = pl.ds(pl.multiple_of(start_x + EDGE, 8), xw), rows
         return remote(
-            bz.at[place, pl.ds(start_x, xw + 2 * EDGE)],
-            bzq.at[me, place],
+            bz.at[place, from_x],
+            bzq.at[me, place, to_x],
             bzq_s.at[other, index],
             bzq_r.at[me, index],
             (other, slab),
         )
 
-    def send(kind):
+    def needed(step, kind):
+        other = lax.rem(me + step, shots)
+        if kind == "left":
+            return other > 0
+        if kind == "right":
+            return other < shots - 1
+        return None
+
+    def send(kind, wait=False):
         for step in range(1, shots):
-            partner_copy(step, kind).start()
+            copy = partner_copy(step, kind)
+            act = copy.wait_send if wait else copy.start
+            need = needed(step, kind)
+            if need is None:
+                act()
+            else:
+                pl.when(need)(act)
 
     send("cnt")
     cntq[me] = cnt[pl.ds(first_x, xw)]
@@ -302,6 +353,7 @@
     loads[1].wait()
     loads[2].wait()
     over(step_zero, 1, chunks - 1)
+    send("bz")
     now_pair.wait_recv()
 
     def ends(body):
@@ -322,11 +374,21 @@
     upc_pair.start()
     bzh_pair = halo(bz, bzh_s, bzh_r)
     bzh_pair.start()
-    send("bz")
+    send("bz_low")
+    send("bz_high")
+    send("left")
+    send("right")
+
+    def send_pz(p):
+        pz_pair(p).start()
+
+    over(send_pz, 0, probes)
     over(step_one, 1, chunks - 1)
+    send("b1")
     upc_pair.wait_recv()
     ends(step_one)
-    send("b1")
+    send("b1_low")
+    send("b1_high")
     bzh_pair.wait_recv()
     send("top")
     send("bottom")
@@ -337,9 +399,22 @@
     own_bz.start()
     own_b1.start()
     loads[3].wait()
-    loads[4].wait()
     px_pair.wait_recv()
-    pz_pair.wait_recv()
+
+    @pl.when(has_left)
+    def _():
+        for p in range(probes):
+            for part in range(2):
+                zs = pl.ds(REACH + part * pair_z, pair_z)
+                pe[p, zs, pl.ds(EDGE - REACH, REACH)] = gotpx[0, p, :, pl.ds(part * REACH, REACH)]
+
+    @pl.when(has_right)
+    def _():
+        for p in range(probes):
+            for part in range(2):
+                zs = pl.ds(REACH + part * pair_z, pair_z)
+                pe[p, zs, pl.ds(EDGE + xw, REACH)] = gotpx[1, p, :, pl.ds(part * REACH, REACH)]
+
     own_bz.wait()
     own_b1.wait()
 
@@ -363,16 +438,22 @@
         @pl.when(t > 0)
         def _():
             start_x = pl.multiple_of(me * xw, 8)
-            whole_x = pl.ds(start_x, xw + 2 * EDGE)
-            for index, place in enumerate((mine, top, bottom)):
+
+            def arrive(index, place, to_x):
                 remote(
-                    bz.at[place, whole_x], bzq.at[shot, place],
+                    bz.at[place, to_x], bzq.at[shot, place, to_x],
                     bzq_s.at[shot, index], bzq_r.at[shot, index], (shot, slab),
                 ).wait_recv()
-            remote(
-                b1.at[:, pl.ds(start_x, xw)], b1q.at[shot],
-                b1q_s.at[shot], b1q_r.at[shot], (shot, slab),
-            ).wait_recv()
+
+            for kind in ("bz", "top", "bottom", "bz_low", "bz_high"):
+                arrive(*ZERO[kind], rows)
+            pl.when(has_left)(lambda: arrive(3, mine, pl.ds(0, EDGE)))
+            pl.when(has_right)(lambda: arrive(4, mine, pl.ds(EDGE + xw, EDGE)))
+            for index, place in ONE.values():
+                remote(
+                    b1.at[place, pl.ds(start_x, xw)], b1q.at[shot, place],
+                    b1q_s.at[shot, index], b1q_r.at[shot, index], (shot, slab),
+                ).wait_recv()
             remote(
                 cnt.at[pl.ds(start_x, xw)], cntq.at[shot], cnt_s.at[shot], cnt_r.at[shot], (shot, slab)
             ).wait_recv()
@@ -380,10 +461,11 @@
         def each_probe(p):
             @pl.when(t == 0)
             def _():
+                pz_pair(p).wait_recv()
                 out_ref[p] = jnp.zeros((nz, xw, ny), jnp.float32)
                 for side in range(2):
                     accz[side, p] = jnp.zeros((REACH, xw, ny), jnp.float32)
-                    accx[side, p] = jnp.zeros((nz, EDGE, ny), jnp.float32)
+                    accx[side, p] = jnp.zeros((nz // 2, EDGE, ny), jnp.float32)
 
             f[top, rows] = pe[p, top, rows] * bzq[shot, top, rows]
             f[bottom, rows] = pe[p, bottom, rows] * bzq[shot, bottom, rows]
@@ -415,13 +497,18 @@
                 zs = pl.ds(z, REACH)
                 ze = pl.ds(REACH + z, REACH)
                 out_ref[p, zs] += bzq[shot, ze, rows] * laplace(w, REACH + z, 2 * EDGE, xw)
-                left_sum = jnp.zeros((REACH, EDGE, ny), jnp.float32)
-                right_sum = jnp.zeros((REACH, EDGE, ny), jnp.float32)
-                for k in range(1, REACH + 1):
-                    left_sum += WEIGHTS[k - 1] * w[ze, pl.ds(EDGE + k, EDGE)]
-                    right_sum += WEIGHTS[k - 1] * w[ze, pl.ds(2 * EDGE + xw - k, EDGE)]
-                accx[0, p, zs] += bzq[shot, ze, pl.ds(0, EDGE)] * left_sum
-                accx[1, p, zs] += bzq[shot, ze, pl.ds(EDGE + xw, EDGE)] * right_sum
+
+            def sideways(c):
+                for part in range(2):
+                    ze = pl.ds(REACH + part * pair_z + c * REACH, REACH)
+                    left_sum = jnp.zeros((REACH, REACH, ny), jnp.float32)
+                    right_sum = jnp.zeros((REACH, REACH, ny), jnp.float32)
+                    for k in range(1, REACH + 1):
+                        left_sum += WEIGHTS[k - 1] * w[ze, pl.ds(EDGE + REACH + k, REACH)]
+                        right_sum += WEIGHTS[k - 1] * w[ze, pl.ds(2 * EDGE + xw - k, REACH)]
+                    place = (p, pl.ds(c * REACH, REACH), pl.ds(part * REACH, REACH))
+                    accx[(0, *place)] += bzq[shot, ze, pl.ds(EDGE - REACH, REACH)] * left_sum
+                    accx[(1, *place)] += bzq[shot, ze, pl.ds(EDGE + xw, REACH)] * right_sum
 
             for j in range(1, REACH + 1):
                 low_sum = jnp.zeros((xw, ny), jnp.float32)
@@ -432,8 +519,9 @@
                 accz[0, p, REACH - j] += bzq[shot, REACH - j, rows] * low_sum
                 accz[1, p, j - 1] += bzq[shot, REACH + nz + j - 1, rows] * high_sum
             pl.when(t == shots - 1)(lambda: cz_pair(p).start())
+            over(sideways, 0, chunks // 2)
+            pl.when(t == shots - 1)(lambda: cx_pair(p).start())
             over(adjoint, 0, chunks)
-            pl.when(t == shots - 1)(lambda: cx_pair(p).start())
 
         over(each_probe, 0, probes)
 
@@ -455,22 +543,26 @@
 
         @pl.when(has_left)
         def _():
-            out_ref[p, :, pl.ds(0, EDGE)] += gotx[0, p]
+            for part in range(2):
+                zs = pl.ds(part * pair_z, pair_z)
+                out_ref[p, zs, pl.ds(0, REACH)] += gotx[0, p, :, pl.ds(part * REACH, REACH)]
 
         @pl.when(has_right)
         def _():
-            out_ref[p, :, pl.ds(xw - EDGE, EDGE)] += gotx[1, p]
+            for part in range(2):
+                zs = pl.ds(part * pair_z, pair_z)
+                out_ref[p, zs, pl.ds(xw - REACH, REACH)] += gotx[1, p, :, pl.ds(part * REACH, REACH)]
 
         out_ref[p] = out_ref[p] * scale
         cz_pair(p).wait_send()
         cx_pair(p).wait_send()
 
     over(finish, 0, probes)
-    for pair in (now_pair, px_pair, pz_pair, upc_pair, bzh_pair):
+    for pair in (now_pair, px_pair, upc_pair, bzh_pair):
         pair.wait_send()
-    for kind in ("cnt", "bz", "b1", "top", "bottom"):
-        for step in range(1, shots):
-            partner_copy(step, kind).wait_send()
+    over(lambda p: pz_pair(p).wait_send(), 0, probes)
+    for kind in ("cnt", *ZERO, *ONE):
+        send(kind, wait=True)
 
 
 def per_device(shots, slabs, *arrays):
@@ -504,20 +596,23 @@
             pltpu.VMEM((tall, xw + 2 * EDGE, ny), f32),
             pltpu.VMEM((tall, xw + 4 * EDGE, ny), f32),
             pltpu.VMEM((2, probes, REACH, xw, ny), f32),
-            pltpu.VMEM((2, probes, nz, EDGE, ny), f32),
+            pltpu.VMEM((2, probes, nz // 2, EDGE, ny), f32),
             pltpu.VMEM((2, probes, REACH, xw, ny), f32),
-            pltpu.VMEM((2, probes, nz, EDGE, ny), f32),
+            pltpu.VMEM((2, probes, nz // 2, EDGE, ny), f32),
+            pltpu.VMEM((2, probes, nz // 2, EDGE, ny), f32),
+            pltpu.VMEM((2, probes, nz // 2, EDGE, ny), f32),
             pltpu.VMEM((2 * ny, ny), jnp.bfloat16),
             dma((7,)),
             *two,
             *two,
             *two,
+            dma((2, probes)),
+            dma((2, probes)),
             *two,
-            *two,
+            dma((shots, 7)),
+            dma((shots, 7)),
             dma((shots, 3)),
             dma((shots, 3)),
-            dma((shots,)),
-            dma((shots,)),
             dma((shots,)),
             dma((shots,)),
             dma((2, probes)),
@@ -526,7 +621,7 @@
             dma((2, probes)),
         ],
         compiler_params=pltpu.CompilerParams(
-            collective_id=0, has_side_effects=True, vmem_limit_bytes=48 * 1024 * 1024
+            collective_id=0, has_side_effects=True, vmem_limit_bytes=63 * 1024 * 1024
         ),
     )(*arrays)
 

time: 72.2 us -> 61.5 us (0.85); the launches traced: 71.1 us -> 61.3 us
  Pallas kernels: 63.4 us -> 56.2 us
  local copies, waits for them, and re-layouts: 5.67 us -> 3.16 us
    pallas_call x1, Pallas kernels: 63.4 us -> 56.2 us  [per_device(): pl.pallas_call(functools.partial(kernel, shots, slabs), out_shape=jax.Sha...]
    unnamed x9 -> x1, local copies, waits for them, and re-layouts: 5.67 us -> 3.16 us
where the time goes in v2:
time: 61.5 us; the launch traced here: 61.3 us
  Pallas kernels  56.2 us (91%)
  local copies, waits for them, and re-layouts  3.16 us (5%)
  between operations  1.95 us (3%)
    pallas_call x1, Pallas kernels, per_device(): pl.pallas_call(functools.partial(kernel, shots, slabs), out_shape=jax.Sha...  56.2 us
    unnamed x1, local copies, waits for them, and re-layouts  3.16 us

profile of v2, /device:TPU:9, one launch (start us, length us, event | category | flops | bytes accessed | tf_op | source)
XLA Modules:
  0.0 61.3 jit_solution(17142444285888426036)
XLA Ops:
  1.9 56.2 %shard_map.82 = f32[4,16,64,128]{3,2,1,0:T(8,128)} custom-call(f32[1,16,128,128]{3,2,1,0:T(8,128)} %prev_ref.1, f32[1,16,128,128]{3,2,1,0:T(8,128)} %now_ref.1, f32[16,128,128]{2,1,0:T(8,128)} %vel_ref.1, f32[4,16,64,128]{3,2,1,0:T(8,128)} %probe_ref.1, s32[1]{0:T(128)S(6)} %copy.10.depth_ref, s32[1]{0:T(128)S(6)} %copy.11.column_ref, ...), custom_call_target="tpu_custom_call" | custom-call | tf_op jit(solution)/shard_map/pallas_call | solution.py:578
  58.2 3.2 %copy.13 = f32[4,16,64,128]{3,2,1,0:T(8,128)} copy(f32[4,16,64,128]{3,2,1,0:T(8,128)} %shard_map.82) | data formatting | bytes 4194304
